TPU v7x, 32 devices: a whole 2x2x4 slice. The times are simulated.
32 devices in a mesh: gz: 4 (over y, core), xy: 8 (over z, x).
Axes of the slice: x: 2, y: 2, z: 4, core: 2. Of those that a mesh axis runs over, the one named last changes fastest.
Arguments:
- cotangent: bfloat16 [4, 8, 9, 128, 128], P('gz', 'xy'), may hold values from -6 to 6
- displacement: float32 [4, 8, 3, 32, 128], P('gz', 'xy'), may hold values from -2 to 2
- neighbours: int32 [4, 8, 32, 128], P('gz', 'xy'), may hold values from 0 to 2303
- counts: int32 [4, 8, 128], P('gz', 'xy'), may hold values from 8 to 32, as said below
- atom_feat: bfloat16 [4, 8, 256, 128], P('gz', 'xy'), may hold values from -6 to 6
- radial_weight: float32 [3, 16, 128], replicated, may hold values from -1.5 to 1.5
- mix_weight: bfloat16 [3, 128, 128], replicated, may hold values from -0.5 to 0.5
Outputs:
- atom_grad: float32 [4, 8, 256, 128], P('gz', 'xy')
- radial_grad: float32 [3, 16, 128], replicated
- mix_grad: float32 [3, 128, 128], replicated
Inputs may be any that keep to these rules, and one draw needn't show every extreme that they name: `counts`: the first probe of the first brick uses all 32 slots and the first probe of the second brick uses 32 // 4.
All inputs are finite; a program needn't handle non-finite values.
Results may differ from a plain program's by a relative error of at most 0.0051.
Values may be sent and summed in bfloat16 or wider, within the bound.
A program may use at most 64 MiB of HBM per device.

v0:
```python
import math
import jax
import jax.numpy as jnp
from jax import lax
from jax.sharding import PartitionSpec as P

CUTOFF = 4.0
LEVEL_SPANS = ((0, 1), (1, 4), (4, 9))


def padded(cells, sides, width):
    for axis, dim in sides:
        count = lax.axis_size(axis)
        head = lax.slice_in_dim(cells, 0, width, axis=dim)
        tail = lax.slice_in_dim(cells, cells.shape[dim] - width, cells.shape[dim], axis=dim)
        cells = jnp.concatenate(
            [
                lax.ppermute(tail, axis, [(i, (i + 1) % count) for i in range(count)]),
                cells,
                lax.ppermute(head, axis, [((i + 1) % count, i) for i in range(count)]),
            ],
            axis=dim,
        )
    return cells


def harmonics(disp):
    scaled = disp / CUTOFF
    coord_x, coord_y, coord_z = (scaled[0], scaled[1], scaled[2])
    root3, root5, root15 = (math.sqrt(3.0), math.sqrt(5.0), math.sqrt(15.0))
    return jnp.stack(
        [
            jnp.ones_like(coord_x),
            root3 * coord_x,
            root3 * coord_y,
            root3 * coord_z,
            root15 * coord_x * coord_y,
            root15 * coord_y * coord_z,
            0.5 * root5 * (2.0 * coord_z * coord_z - coord_x * coord_x - coord_y * coord_y),
            root15 * coord_x * coord_z,
            0.5 * root15 * (coord_x * coord_x - coord_y * coord_y),
        ]
    )


def basis(disp, nbasis):
    distance = jnp.sqrt(jnp.sum(disp * disp, axis=0))
    centres = jnp.arange(nbasis).astype(jnp.float32) * (CUTOFF / (nbasis - 1))
    sharpness = ((nbasis - 1) / CUTOFF) ** 2
    envelope = 0.5 * (jnp.cos(math.pi * distance / CUTOFF) + 1.0)
    shaped = centres.reshape((nbasis,) + (1,) * distance.ndim)
    return jnp.exp(-sharpness * (distance[None] - shaped) ** 2) * envelope[None]


def exact(form, left, right):
    return jnp.einsum(form, left, right, precision=lax.Precision.HIGHEST)


def matmul(form, left, right):
    return jnp.einsum(form, left, right, preferred_element_type=jnp.float32)


def gate_backward(moments, mix_weight, cotangent):
    mixed_out = [
        matmul("mpc,cd->mpd", moments[span_start:span_end], mix_weight[level])
        for level, (span_start, span_end) in enumerate(LEVEL_SPANS)
    ]
    scalar = mixed_out[0][0]
    gating = jax.nn.sigmoid(scalar)
    gate_slope = gating * (1.0 - gating)
    cot_float = cotangent.astype(jnp.float32)
    higher = jnp.concatenate(mixed_out[1:], 0)
    first_term = (
        cot_float[0] * (gating + scalar * gate_slope)
        + jnp.sum(cot_float[1:] * higher, 0) * gate_slope
    )
    dmixed = jnp.concatenate([first_term[None], cot_float[1:] * gating[None]], 0).astype(
        jnp.bfloat16
    )
    dmoments = jnp.concatenate(
        [
            matmul("mpd,cd->mpc", dmixed[span_start:span_end], mix_weight[level])
            for level, (span_start, span_end) in enumerate(LEVEL_SPANS)
        ],
        0,
    ).astype(jnp.bfloat16)
    mix_part = jnp.stack(
        [
            matmul("mpc,mpd->cd", moments[span_start:span_end], dmixed[span_start:span_end])
            for span_start, span_end in LEVEL_SPANS
        ]
    )
    return (dmoments, mix_part)


def shards(cotangent, displacement, neighbours, counts, atom_feat, radial_weight, mix_weight):
    cot_local = cotangent[0, 0]
    disp_local = displacement[0, 0]
    neighbour_local_index = neighbours[0, 0]
    probe_tally = counts[0, 0]
    slot_count = neighbour_local_index.shape[0]
    probe_count = neighbour_local_index.shape[1]
    natom = atom_feat.shape[2]
    channels = atom_feat.shape[3]
    nbasis = radial_weight.shape[1]
    filled_slots = (
        lax.broadcasted_iota(jnp.int32, (slot_count, probe_count), 0) < probe_tally[None]
    ).astype(jnp.float32)
    angular = harmonics(disp_local) * filled_slots[None]
    radial_basis = basis(disp_local, nbasis)
    atom_table = padded(atom_feat, (("gz", 0), ("xy", 1)), 1).reshape(9 * natom, channels)
    features = atom_table[neighbour_local_index].astype(jnp.float32)
    radial = exact("bkp,lbc->lkpc", radial_basis, radial_weight)
    pieces = []
    for level, (span_start, span_end) in enumerate(LEVEL_SPANS):
        weighted = radial[level] * features
        pieces.append(jnp.sum(angular[span_start:span_end, :, :, None] * weighted[None], axis=1))
    moments = jnp.concatenate(pieces, 0).astype(jnp.bfloat16)
    dmoments, mix_part = gate_backward(moments, mix_weight, cot_local)
    mix_total = lax.psum(mix_part, ("gz", "xy"))
    dmoment_float = dmoments.astype(jnp.float32)
    contrib = jnp.zeros(features.shape, jnp.float32)
    radial_parts = []
    for level, (span_start, span_end) in enumerate(LEVEL_SPANS):
        traced = jnp.sum(
            angular[span_start:span_end, :, :, None] * dmoment_float[span_start:span_end, None],
            axis=0,
        )
        contrib = contrib + radial[level] * traced
        radial_parts.append(exact("bkp,kpc->bc", radial_basis, features * traced))
    grads = (
        jnp.zeros((9 * natom, channels), jnp.float32)
        .at[neighbour_local_index.reshape(-1)]
        .add(contrib.reshape(-1, channels))
    )
    radial_part = jnp.stack(radial_parts)
    radial_total = lax.psum(radial_part, ("gz", "xy"))
    blocks = grads.reshape(3, 3, natom, channels)
    outer_rows = jnp.stack([blocks[0], blocks[2]], 0)
    arrived = padded(outer_rows, (("gz", 0),), 1)
    columns = blocks[1] + arrived[0] + arrived[3]
    outer_columns = jnp.stack([columns[0], columns[2]], 0)
    landed = padded(outer_columns, (("xy", 0),), 1)
    owned = columns[1] + landed[0] + landed[3]
    return (owned[None, None], radial_total, mix_total)


def solution(mesh):
    in_specs = (
        P("gz", "xy", None, None, None),
        P("gz", "xy", None, None, None),
        P("gz", "xy", None, None),
        P("gz", "xy", None),
        P("gz", "xy", None, None),
        P(),
        P(),
    )
    out_specs = (P("gz", "xy", None, None), P(), P())
    return jax.shard_map(shards, mesh=mesh, in_specs=in_specs, out_specs=out_specs, check_vma=False)
```

profile of v0, /device:TPU:10, one launch (start us, length us, event | category | flops | bytes accessed | tf_op | source)
XLA Modules:
  0.0 237.2 jit_solution(9430039311791269466)
XLA Ops:
  7.2 0.0 all-reduce.2.cloned.1.call-start
  7.2 0.1 collective-permute-start
  7.3 1.7 collective-permute-start.1
  9.0 0.8 multiply_reduce_fusion.5
  9.9 0.7 fusion.78
  10.6 0.1 fusion.86
  10.7 1.3 compare_select_fusion
  12.1 7.2 %convolution_bitcast_fusion = f32[3,32,128,128]{3,2,0,1:T(8,128)} fusion(f32[32,128]{1,0:T(8,128)S(1)} %get-tuple-element.23, f32[16]{0:T(128)S(1)} %convert_multiply_fusion, f32[32,128]{1,0:T(8,128)S(1)} %get-tuple-element.22, f32[3,16,128]{2,1,0:T(8,128)S(1)} %copy-done), kind=kOutput, calls=%fused_computation.6 | convolution fusion | flops 302252032 | bytes 6348864 | tf_op jit(solution)/shard_map/bkp,lbc->lkpc/dot_general | solution.py:56
  19.4 0.9 convert_element_type.43
  20.3 1.6 collective-permute-start.2
  21.9 0.5 collective-permute-start.3
  22.4 8.9 %collective-permute-done.2 = bf16[3,1,256,128]{3,2,1,0:T(8,128)(2,1)S(1)} collective-permute-done((bf16[3,1,256,128]{3,2,1,0:T(8,128)(2,1)S(1)}, bf16[3,1,256,128]{3,2,1,0:T(8,128)(2,1)S(1)}, u32[]{:S(2)}, u32[]{:S(2)}) %collective-permute-start.2) | collective-permute-done | bytes 196640 | tf_op jit(solution)/shard_map/ppermute | solution.py:18
  31.3 0.1 pad_maximum_fusion
  31.4 12.1 %gather_fusion = bf16[4096,128]{1,0:T(8,128)(2,1)S(1)} fusion(bf16[2304,128]{1,0:T(8,128)(2,1)S(1)} %bitcast.167, s32[4096]{0:T(1024)S(1)} %fusion.74), kind=kCustom, calls=%fused_computation | custom fusion | bytes 2113536 | tf_op jit(solution)/shard_map/gather | solution.py:112
  43.5 0.1 convert_element_type.49
  43.7 3.6 %fusion.83 = (f32[1,32,128,128]{3,2,0,1:T(8,128)S(1)}, bf16[128,128]{1,0:T(8,128)(2,1)S(1)}, f32[32,128,128]{2,1,0:T(8,128)S(1)}, f32[32,128,128]{2,1,0:T(8,128)...) fusion(f32[3,32,128,128]{3,2,0,1:T(8,128)} %convolution_bitcast_fusion, ...), kind=kLoop, calls=%fused_computation.141 | loop fusion | flops 3129344 | bytes 19972096 | tf_op jit(solution)/shard_map/slice | solution.py:129
  47.3 2.0 multiply_reduce_fusion.3
  49.3 0.1 fusion.54
  49.4 3.1 %multiply_reduce_fusion.1 = bf16[5,128,128]{2,1,0:T(8,128)(2,1)S(1)} fusion(f32[32,128,128]{2,1,0:T(8,128)S(1)} %get-tuple-element.7, f32[5,32,128]{2,1,0:T(8,128)S(1)} %slice.162), kind=kLoop, calls=%fused_computation.3 | loop fusion | flops 5160960 | bytes 2342912 | tf_op jit(solution)/shard_map/reduce_sum | solution.py:117
  52.6 0.2 fusion.48
  52.7 0.2 add_divide_fusion
  52.9 0.1 fusion.24
  53.0 0.2 convolution_bitcast_fusion.2
  53.2 0.2 convolution_bitcast_fusion.1
  53.5 0.2 convolution_convert_fusion
  53.7 0.2 convolution_convert_fusion.1
  53.9 0.1 fusion.52
  53.9 0.1 fusion.10
  54.1 2.1 multiply_reduce_fusion.2
  56.3 2.1 fusion.11
  58.4 2.0 fusion.14
  60.4 3.2 %multiply_reduce_fusion = f32[32,128,128]{2,1,0:T(8,128)S(1)} fusion(f32[5,128,128]{2,1,0:T(8,128)S(1)} %fusion.27, f32[5,32,128]{2,1,0:T(8,128)S(1)} %slice.162), kind=kLoop, calls=%fused_computation.2 | loop fusion | flops 4718592 | bytes 2506752 | tf_op jit(solution)/shard_map/reduce_sum | solution.py:125
  63.6 2.4 %fusion = f32[4096,128]{1,0:T(8,128)} fusion(f32[32,128,128]{2,1,0:T(8,128)S(1)} %multiply_reduce_fusion, f32[1,32,128,128]{3,2,0,1:T(8,128)S(1)} %get-tuple-element.9, f32[32,128,128]{2,1,0:T(8,128)S(1)} %multiply_reduce_fusion.2, f32[1,32,128,128]{3,2,0,1:T(8,128)S(1)} %get-tuple-element.10, f32[1,32,128,128]{3,2,0,1:T(8,128)S(1)} %get-tuple-element.5, ...), kind=kLoop, calls=%fused_computation.8 | loop fusion | flops 3145728 | bytes 12664832 | tf_op jit(solution)/shard_map/add | solution.py:129
  66.1 22.9 %scatter_custom_fusion = f32[2304,128]{1,0:T(8,128)S(1)} fusion(s32[4096]{0:T(1024)} %bitcast.176, f32[4096,128]{1,0:T(8,128)} %fusion, f32[]{:T(128)} %constant.14.clone.1), kind=kCustom, calls=%fused_computation.36 | custom fusion | flops 524288 | bytes 1180160 | tf_op jit(solution)/shard_map/scatter-add | solution.py:134
  89.0 0.1 fusion.84
  89.1 0.1 collective-permute-start.4
  89.2 1.7 collective-permute-start.5
  90.9 0.2 convolution_bitcast_fusion.3
  91.1 1.3 fusion.17
  92.5 7.3 %collective-permute-done.4 = f32[1,3,256,128]{3,2,1,0:T(8,128)S(1)} collective-permute-done((f32[1,3,256,128]{3,2,1,0:T(8,128)S(1)}, f32[1,3,256,128]{3,2,1,0:T(8,128)S(1)}, u32[]{:S(2)}, u32[]{:S(2)}) %collective-permute-start.4) | collective-permute-done | bytes 393248 | tf_op jit(solution)/shard_map/ppermute | solution.py:18
  99.8 0.1 bitcast_add_fusion
  99.9 2.5 %collective-permute-start.6 = (f32[1,256,128]{2,1,0:T(8,128)S(1)}, f32[1,256,128]{2,1,0:T(8,128)S(1)}, u32[]{:S(2)}, u32[]{:S(2)}) collective-permute-start(f32[1,256,128]{2,1,0:T(8,128)S(1)} %get-tuple-element.16), channel_id=1, source_target_pairs={{0,1},{1,2},{2,3},{3,4},{4,5},{5,6},{6,7},{7,0},{8,9},{9,10},{10,1... | collective-permute-start | bytes 393224 | tf_op jit(solution)/shard_map/ppermute | solution.py:18
  102.4 0.7 pad_maximum_fusion.1
  103.1 0.0 all-reduce.2.cloned.1.call-update
  103.1 43.0 %psum.14 = f32[3,16,128]{2,1,0:T(8,128)} all-reduce(f32[3,16,128]{2,1,0:T(8,128)S(1)} %pad_maximum_fusion.4), channel_id=1, replica_groups=mesh['gz'=4,'xy'=8] {'gz','xy'}, use_global_device_ids=true, to_apply=%region_8.0 | all-reduce | flops 6144 | bytes 49152 | tf_op jit(solution)/shard_map/psum | solution.py:137
  146.1 0.7 fusion.29
  146.8 81.9 %all-reduce.2.cloned.1.call-done = f32[3,128,128]{2,1,0:T(8,128)} async-done(((f32[3,128,128]{2,1,0:T(8,128)}), f32[3,128,128]{2,1,0:T(8,128)}) %all-reduce.2.cloned.1.call-update) | async-done | bytes 196624 | tf_op jit(solution)/shard_map/psum | solution.py:120
  228.7 1.6 copy.28
  (56 shorter events, 0.3 us)
Async XLA Ops:
  7.2 4.9 %copy-start = (f32[3,16,128]{2,1,0:T(8,128)S(1)}, f32[3,16,128]{2,1,0:T(8,128)}, u32[]{:S(2)}) copy-start(f32[3,16,128]{2,1,0:T(8,128)} %param.12) | copy-start | bytes 73732
  7.2 221.5 %all-reduce.2.cloned.1.call-start = ((), (), s32[]{:S(2)}) async-start(), calls=%async_computation | async-start | bytes 393216 | tf_op jit(solution)/shard_map/psum | solution.py:120
  7.2 13.0 %collective-permute-start = (bf16[1,1,256,128]{3,2,1,0:T(8,128)(2,1)}, bf16[1,1,256,128]{3,2,1,0:T(8,128)(2,1)S(1)}, u32[]{:S(2)}, u32[]{:S(2)}) collective-permute-start(bf16[1,1,256,128]{3,2,1,0:T(8,128)(2,1)} %param.11), channel_id=1, source_target_pairs={{0,8},{8,16},{16,24},{24,0},{1,9},{9,17},{17,25},{25,1},{2,10},{10... | collective-permute-start | bytes 196616 | tf_op jit(solution)/shard_map/ppermute | solution.py:18
  7.3 13.0 %collective-permute-start.1 = (bf16[1,1,256,128]{3,2,1,0:T(8,128)(2,1)}, bf16[1,1,256,128]{3,2,1,0:T(8,128)(2,1)S(1)}, u32[]{:S(2)}, u32[]{:S(2)}) collective-permute-start(bf16[1,1,256,128]{3,2,1,0:T(8,128)(2,1)} %param.11), channel_id=1, source_target_pairs={{8,0},{16,8},{24,16},{0,24},{9,1},{17,9},{25,17},{1,25},{10,2},{18... | collective-permute-start | bytes 196616 | tf_op jit(solution)/shard_map/ppermute | solution.py:20
  9.0 47.2 %copy-start.11 = (f32[16]{0:T(128)}, f32[16]{0:T(128)S(1)}, u32[]{:S(2)}) copy-start(f32[16]{0:T(128)S(1)} %convert_multiply_fusion) | copy-start | bytes 196
  12.1 7.3 %copy-start.4 = (bf16[1,1,9,128,128]{4,3,2,1,0:T(8,128)(2,1)S(1)}, bf16[1,1,9,128,128]{4,3,2,1,0:T(8,128)(2,1)}, u32[]{:S(2)}) copy-start(bf16[1,1,9,128,128]{4,3,2,1,0:T(8,128)(2,1)} %param.7) | copy-start | bytes 884740
  12.1 8.2 %copy-start.6 = (bf16[1,1,256,128]{3,2,1,0:T(8,128)(2,1)S(1)}, bf16[1,1,256,128]{3,2,1,0:T(8,128)(2,1)}, u32[]{:S(2)}) copy-start(bf16[1,1,256,128]{3,2,1,0:T(8,128)(2,1)} %param.11) | copy-start | bytes 196612
  12.1 10.3 %copy-start.7 = (s32[1,1,32,128]{3,2,1,0:T(8,128)S(1)}, s32[1,1,32,128]{3,2,1,0:T(8,128)}, u32[]{:S(2)}) copy-start(s32[1,1,32,128]{3,2,1,0:T(8,128)} %param.9) | copy-start | bytes 49156
  19.3 24.3 %copy-start.8 = (f32[32,128]{1,0:T(8,128)}, f32[32,128]{1,0:T(8,128)S(1)}, u32[]{:S(2)}) copy-start(f32[32,128]{1,0:T(8,128)S(1)} %get-tuple-element.19) | copy-start | bytes 49156
  20.3 11.0 %collective-permute-start.2 = (bf16[3,1,256,128]{3,2,1,0:T(8,128)(2,1)S(1)}, bf16[3,1,256,128]{3,2,1,0:T(8,128)(2,1)S(1)}, u32[]{:S(2)}, u32[]{:S(2)}) collective-permute-start(bf16[3,1,256,128]{3,2,1,0:T(8,128)(2,1)S(1)} %constant_dynamic-update-slice_fusion.9), channel_id=1, source_target_pairs={{0,1},{1,2},{2,3},{3,4},{4,5},{5,6},{6,7},{7,0},{8,9},{9,10},{10,1... | collective-permute-start | bytes 589832 | tf_op jit(solution)/shard_map/ppermute | solution.py:18
  21.9 9.4 %collective-permute-start.3 = (bf16[3,1,256,128]{3,2,1,0:T(8,128)(2,1)S(1)}, bf16[3,1,256,128]{3,2,1,0:T(8,128)(2,1)S(1)}, u32[]{:S(2)}, u32[]{:S(2)}) collective-permute-start(bf16[3,1,256,128]{3,2,1,0:T(8,128)(2,1)S(1)} %constant_dynamic-update-slice_fusion.9), channel_id=1, source_target_pairs={{1,0},{2,1},{3,2},{4,3},{5,4},{6,5},{7,6},{0,7},{9,8},{10,9},{11,1... | collective-permute-start | bytes 589832 | tf_op jit(solution)/shard_map/ppermute | solution.py:20
  47.3 2.0 copy-start.5
  49.3 3.6 %copy-start.3 = (f32[1,1,9,128,128]{4,3,2,1,0:T(8,128)S(1)}, f32[1,1,9,128,128]{4,3,2,1,0:T(8,128)}, u32[]{:S(2)}) copy-start(f32[1,1,9,128,128]{4,3,2,1,0:T(8,128)} %convert_element_type.43) | copy-start | bytes 1769476
  53.9 2.4 %copy-start.9 = (f32[32,128]{1,0:T(8,128)S(1)}, f32[32,128]{1,0:T(8,128)}, u32[]{:S(2)}) copy-start(f32[32,128]{1,0:T(8,128)} %copy-done.8) | copy-start | bytes 49156
  63.6 2.4 %copy-start.1 = (f32[32,128,128]{2,1,0:T(8,128)}, f32[32,128,128]{2,1,0:T(8,128)S(1)}, u32[]{:S(2)}) copy-start(f32[32,128,128]{2,1,0:T(8,128)S(1)} %multiply_reduce_fusion) | copy-start | bytes 6291460
  66.1 25.0 %copy-start.12 = (f32[16]{0:T(128)S(1)}, f32[16]{0:T(128)}, u32[]{:S(2)}) copy-start(f32[16]{0:T(128)} %copy-done.11) | copy-start | bytes 196
  89.0 2.1 copy-start.2
  89.1 10.7 %collective-permute-start.4 = (f32[1,3,256,128]{3,2,1,0:T(8,128)S(1)}, f32[1,3,256,128]{3,2,1,0:T(8,128)S(1)}, u32[]{:S(2)}, u32[]{:S(2)}) collective-permute-start(f32[1,3,256,128]{3,2,1,0:T(8,128)S(1)} %bitcast.174), channel_id=1, source_target_pairs={{0,8},{8,16},{16,24},{24,0},{1,9},{9,17},{17,25},{25,1},{2,10},{10... | collective-permute-start | bytes 1179656 | tf_op jit(solution)/shard_map/ppermute | solution.py:18
  89.2 10.6 %collective-permute-start.5 = (f32[1,3,256,128]{3,2,1,0:T(8,128)S(1)}, f32[1,3,256,128]{3,2,1,0:T(8,128)S(1)}, u32[]{:S(2)}, u32[]{:S(2)}) collective-permute-start(f32[1,3,256,128]{3,2,1,0:T(8,128)S(1)} %bitcast.173), channel_id=1, source_target_pairs={{8,0},{16,8},{24,16},{0,24},{9,1},{17,9},{25,17},{1,25},{10,2},{18... | collective-permute-start | bytes 1179656 | tf_op jit(solution)/shard_map/ppermute | solution.py:20
  92.5 10.6 %copy-start.10 = (f32[1,16,128]{2,1,0:T(8,128)S(1)}, f32[1,16,128]{2,1,0:T(8,128)}, u32[]{:S(2)}) copy-start(f32[1,16,128]{2,1,0:T(8,128)} %fusion.11) | copy-start | bytes 24580
  99.9 46.2 %collective-permute-start.6 = (f32[1,256,128]{2,1,0:T(8,128)S(1)}, f32[1,256,128]{2,1,0:T(8,128)S(1)}, u32[]{:S(2)}, u32[]{:S(2)}) collective-permute-start(f32[1,256,128]{2,1,0:T(8,128)S(1)} %get-tuple-element.16), channel_id=1, source_target_pairs={{0,1},{1,2},{2,3},{3,4},{4,5},{5,6},{6,7},{7,0},{8,9},{9,10},{10,1... | collective-permute-start | bytes 393224 | tf_op jit(solution)/shard_map/ppermute | solution.py:18
  102.4 43.7 %collective-permute-start.7 = (f32[1,256,128]{2,1,0:T(8,128)S(1)}, f32[1,256,128]{2,1,0:T(8,128)S(1)}, u32[]{:S(2)}, u32[]{:S(2)}) collective-permute-start(f32[1,256,128]{2,1,0:T(8,128)S(1)} %get-tuple-element.17), channel_id=1, source_target_pairs={{1,0},{2,1},{3,2},{4,3},{5,4},{6,5},{7,6},{0,7},{9,8},{10,9},{11,1... | collective-permute-start | bytes 393224 | tf_op jit(solution)/shard_map/ppermute | solution.py:20
Sparse Core Ops, SparseCore 0:
  103.2 125.4 all-reduce.1
where the time goes:
time: 238 us; the launch traced here: 237 us
  waiting for transfers between devices  98.2 us (41%)
  other arithmetic  45.1 us (19%)
  blocking collectives  43 us (18%)
  between operations  14.5 us (6%)
  matrix products  14.3 us (6%)
  local copies, waits for them, and re-layouts  14 us (6%)
  starting transfers between devices  8.19 us (3%)
    psum x1, waiting for transfers between devices, shards(): mix_total = lax.psum(mix_part, ('gz', 'xy'))  81.9 us
    psum x1, blocking collectives, shards(): radial_total = lax.psum(radial_part, ('gz', 'xy'))  43 us
    scatter-add x1, other arithmetic, shards(): grads = jnp.zeros((9 * natom, channels), jnp.float32).at[neighbour_local_...  22.9 us
    ppermute x4, waiting for transfers between devices, padded(): lax.ppermute(tail, axis, [(i, (i + 1) % count) for i in range(count)])  16.2 us
    dot_general x4, matrix products, exact(): return jnp.einsum(form, left, right, precision=lax.Precision.HIGHEST)  12.7 us
    gather x1, local copies, waits for them, and re-layouts, shards(): features = atom_table[neighbour_local_index].astype(jnp.float32)  12.1 us
    reduce_sum x2, other arithmetic, shards(): jnp.sum(angular[span_start:span_end, :, :, None] * dmoment_float[span_sta...  5.34 us
    reduce_sum x2, other arithmetic, shards(): jnp.sum(angular[span_start:span_end, :, :, None] * weighted[None], axis=1)  5.1 us
  transfers between devices with their start and end apart: 9, of which 3 were waited for; matrix products, arithmetic and copies ran while one was open for 6% of the time, Pallas kernels for 0%

commit v1 on v0

--- a/solution.py
+++ b/solution.py
@@ -117,7 +117,8 @@
         pieces.append(jnp.sum(angular[span_start:span_end, :, :, None] * weighted[None], axis=1))
     moments = jnp.concatenate(pieces, 0).astype(jnp.bfloat16)
     dmoments, mix_part = gate_backward(moments, mix_weight, cot_local)
-    mix_total = lax.psum(mix_part, ("gz", "xy"))
+    parts = lax.all_gather(mix_part, ("gz", "xy"))
+    mix_total = jnp.sum(parts, axis=0)
     dmoment_float = dmoments.astype(jnp.float32)
     contrib = jnp.zeros(features.shape, jnp.float32)
     radial_parts = []

time: 238 us -> 157 us (0.66)
  waiting for transfers between devices: 98.2 us -> 14.8 us
  other arithmetic: 45.1 us -> 49.1 us
    psum x1 -> x0, waiting for transfers between devices: 81.9 us -> none  [shards(): mix_total = lax.psum(mix_part, ('gz', 'xy'))]
    reduce_sum x0 -> x1, other arithmetic: none -> 3.78 us  [shards(): mix_total = jnp.sum(parts, axis=0)]
  transfers between devices with their start and end apart: 9 -> 9, of which waited for: 3 -> 2; matrix products, arithmetic and copies ran while one was open for 6% -> 30% of each run, Pallas kernels for 0% -> 0%
where the time goes in v1:
time: 157 us; the launch traced here: 156 us
  other arithmetic  49.1 us (31%)
  blocking collectives  43.6 us (28%)
  waiting for transfers between devices  14.8 us (9%)
  between operations  14.5 us (9%)
  matrix products  13 us (8%)
  local copies, waits for them, and re-layouts  12.6 us (8%)
  starting transfers between devices  8.21 us (5%)
    psum x1, blocking collectives, shards(): radial_total = lax.psum(radial_part, ('gz', 'xy'))  43.6 us
    scatter-add x1, other arithmetic, shards(): grads = jnp.zeros((9 * natom, channels), jnp.float32).at[neighbour_local_...  23 us
    ppermute x4, waiting for transfers between devices, padded(): lax.ppermute(tail, axis, [(i, (i + 1) % count) for i in range(count)])  14.8 us
    gather x1, local copies, waits for them, and re-layouts, shards(): features = atom_table[neighbour_local_index].astype(jnp.float32)  12.1 us
    dot_general x4, matrix products, exact(): return jnp.einsum(form, left, right, precision=lax.Precision.HIGHEST)  11.3 us
    reduce_sum x2, other arithmetic, shards(): jnp.sum(angular[span_start:span_end, :, :, None] * dmoment_float[span_sta...  5.33 us
    reduce_sum x2, other arithmetic, shards(): jnp.sum(angular[span_start:span_end, :, :, None] * weighted[None], axis=1)  5.1 us
    slice x1, other arithmetic, shards(): contrib = contrib + radial[level] * traced  5.07 us
  transfers between devices with their start and end apart: 9, of which 2 were waited for; matrix products, arithmetic and copies ran while one was open for 30% of the time, Pallas kernels for 0%

profile of v1, /device:TPU:10, one launch (start us, length us, event | category | flops | bytes accessed | tf_op | source)
XLA Modules:
  0.0 155.8 jit_solution(9148573011479387827)
XLA Ops:
  7.2 0.0 copy-start
  7.2 0.0 all-gather.3.cloned.1.call-start
  7.2 0.1 collective-permute-start
  7.3 1.7 %collective-permute-start.1 = (bf16[1,1,256,128]{3,2,1,0:T(8,128)(2,1)}, bf16[1,1,256,128]{3,2,1,0:T(8,128)(2,1)S(1)}, u32[]{:S(2)}, u32[]{:S(2)}) collective-permute-start(bf16[1,1,256,128]{3,2,1,0:T(8,128)(2,1)} %param.11), channel_id=1, source_target_pairs={{8,0},{16,8},{24,16},{0,24},{9,1},{17,9},{25,17},{1,25},{10,2},{18... | collective-permute-start | bytes 196616 | tf_op jit(solution)/shard_map/ppermute | solution.py:20
  9.0 0.8 multiply_reduce_fusion.5
  9.9 0.7 fusion.78
  10.6 0.1 fusion.86
  10.8 7.2 %convolution_bitcast_fusion = f32[3,32,128,128]{3,2,0,1:T(8,128)} fusion(f32[32,128]{1,0:T(8,128)S(1)} %get-tuple-element.23, f32[16]{0:T(128)S(1)} %convert_multiply_fusion, f32[32,128]{1,0:T(8,128)S(1)} %get-tuple-element.22, f32[3,16,128]{2,1,0:T(8,128)S(1)} %copy-done), kind=kOutput, calls=%fused_computation.6 | convolution fusion | flops 302252032 | bytes 6348864 | tf_op jit(solution)/shard_map/bkp,lbc->lkpc/dot_general | solution.py:56
  18.0 0.9 convert_element_type.43
  19.0 1.6 %collective-permute-start.2 = (bf16[3,1,256,128]{3,2,1,0:T(8,128)(2,1)S(1)}, bf16[3,1,256,128]{3,2,1,0:T(8,128)(2,1)S(1)}, u32[]{:S(2)}, u32[]{:S(2)}) collective-permute-start(bf16[3,1,256,128]{3,2,1,0:T(8,128)(2,1)S(1)} %constant_dynamic-update-slice_fusion.9), channel_id=1, source_target_pairs={{0,1},{1,2},{2,3},{3,4},{4,5},{5,6},{6,7},{7,0},{8,9},{9,10},{10,1... | collective-permute-start | bytes 589832 | tf_op jit(solution)/shard_map/ppermute | solution.py:18
  20.6 0.5 collective-permute-start.3
  21.1 8.9 %collective-permute-done.2 = bf16[3,1,256,128]{3,2,1,0:T(8,128)(2,1)S(1)} collective-permute-done((bf16[3,1,256,128]{3,2,1,0:T(8,128)(2,1)S(1)}, bf16[3,1,256,128]{3,2,1,0:T(8,128)(2,1)S(1)}, u32[]{:S(2)}, u32[]{:S(2)}) %collective-permute-start.2) | collective-permute-done | bytes 196640 | tf_op jit(solution)/shard_map/ppermute | solution.py:18
  29.9 0.1 pad_maximum_fusion
  30.0 12.1 %gather_fusion = bf16[4096,128]{1,0:T(8,128)(2,1)S(1)} fusion(bf16[2304,128]{1,0:T(8,128)(2,1)S(1)} %bitcast.168, s32[4096]{0:T(1024)S(1)} %fusion.74), kind=kCustom, calls=%fused_computation | custom fusion | bytes 2113536 | tf_op jit(solution)/shard_map/gather | solution.py:112
  42.2 0.1 convert_element_type.49
  42.3 5.1 %fusion.83 = (f32[1,32,128,128]{3,2,0,1:T(8,128)}, bf16[128,128]{1,0:T(8,128)(2,1)S(1)}, f32[32,128,128]{2,1,0:T(8,128)S(1)}, f32[32,128,128]{2,1,0:T(8,128)S(1)...) fusion(f32[3,32,128,128]{3,2,0,1:T(8,128)} %convolution_bitcast_fusion, ...), kind=kLoop, calls=%fused_computation.141 | loop fusion | flops 3129344 | bytes 19972096 | tf_op jit(solution)/shard_map/slice | solution.py:130
  47.4 2.0 %multiply_reduce_fusion.3 = bf16[3,128,128]{2,1,0:T(8,128)(2,1)S(1)} fusion(f32[32,128,128]{2,1,0:T(8,128)S(1)} %get-tuple-element.8, f32[3,32,128]{2,1,0:T(8,128)S(1)} %slice.160), kind=kLoop, calls=%fused_computation.5 | loop fusion | flops 3096576 | bytes 2244608 | tf_op jit(solution)/shard_map/reduce_sum | solution.py:117
  49.4 0.1 fusion.54
  49.5 3.1 %multiply_reduce_fusion.1 = bf16[5,128,128]{2,1,0:T(8,128)(2,1)S(1)} fusion(f32[32,128,128]{2,1,0:T(8,128)S(1)} %get-tuple-element.7, f32[5,32,128]{2,1,0:T(8,128)S(1)} %slice.162), kind=kLoop, calls=%fused_computation.3 | loop fusion | flops 5160960 | bytes 2342912 | tf_op jit(solution)/shard_map/reduce_sum | solution.py:117
  52.7 0.2 fusion.48
  52.8 0.2 add_divide_fusion
  53.0 0.1 fusion.24
  53.1 0.2 convolution_bitcast_fusion.2
  53.3 0.2 convolution_bitcast_fusion.1
  53.6 0.1 fusion.52
  53.6 0.2 convolution_bitcast_fusion.3
  53.8 0.7 pad_maximum_fusion.1
  54.5 0.0 all-gather.3.cloned.1.call-update
  54.6 0.1 fusion.10
  54.7 0.2 convolution_convert_fusion.1
  54.9 0.2 convolution_convert_fusion
  55.2 2.1 %multiply_reduce_fusion.2 = f32[32,128,128]{2,1,0:T(8,128)S(1)} fusion(f32[3,128,128]{2,1,0:T(8,128)S(1)} %maximum_convert_fusion, f32[3,32,128]{2,1,0:T(8,128)S(1)} %slice.160), kind=kLoop, calls=%fused_computation.4 | loop fusion | flops 2621440 | bytes 2342912 | tf_op jit(solution)/shard_map/reduce_sum | solution.py:126
  57.4 3.2 %multiply_reduce_fusion = f32[32,128,128]{2,1,0:T(8,128)S(1)} fusion(f32[5,128,128]{2,1,0:T(8,128)S(1)} %fusion.27, f32[5,32,128]{2,1,0:T(8,128)S(1)} %slice.162), kind=kLoop, calls=%fused_computation.2 | loop fusion | flops 4718592 | bytes 2506752 | tf_op jit(solution)/shard_map/reduce_sum | solution.py:126
  60.6 2.4 %fusion = f32[4096,128]{1,0:T(8,128)} fusion(f32[32,128,128]{2,1,0:T(8,128)S(1)} %multiply_reduce_fusion, f32[1,32,128,128]{3,2,0,1:T(8,128)S(1)} %copy-done.6, f32[32,128,128]{2,1,0:T(8,128)S(1)} %multiply_reduce_fusion.2, f32[1,32,128,128]{3,2,0,1:T(8,128)S(1)} %copy-done.7, f32[1,32,128,128]{3,2,0,1:T(8,128)S(1)} %copy-done.5, ...), kind=kLoop, calls=%fused_computation.8 | loop fusion | flops 3145728 | bytes 12664832 | tf_op jit(solution)/shard_map/add | solution.py:130
  63.1 23.0 %scatter_custom_fusion = f32[2304,128]{1,0:T(8,128)S(1)} fusion(s32[4096]{0:T(1024)S(1)} %bitcast.178, f32[4096,128]{1,0:T(8,128)} %fusion, f32[]{:T(128)} %constant.14.clone.1), kind=kCustom, calls=%fused_computation.36 | custom fusion | flops 524288 | bytes 1180160 | tf_op jit(solution)/shard_map/scatter-add | solution.py:135
  86.1 0.1 fusion.84
  86.1 0.1 collective-permute-start.4
  86.2 1.7 %collective-permute-start.5 = (f32[1,3,256,128]{3,2,1,0:T(8,128)S(1)}, f32[1,3,256,128]{3,2,1,0:T(8,128)S(1)}, u32[]{:S(2)}, u32[]{:S(2)}) collective-permute-start(f32[1,3,256,128]{3,2,1,0:T(8,128)S(1)} %bitcast.175), channel_id=1, source_target_pairs={{8,0},{16,8},{24,16},{0,24},{9,1},{17,9},{25,17},{1,25},{10,2},{18... | collective-permute-start | bytes 1179656 | tf_op jit(solution)/shard_map/ppermute | solution.py:20
  87.9 1.3 fusion.14
  89.3 0.3 copy-done.4
  89.5 1.3 fusion.17
  90.9 5.9 %collective-permute-done.4 = f32[1,3,256,128]{3,2,1,0:T(8,128)S(1)} collective-permute-done((f32[1,3,256,128]{3,2,1,0:T(8,128)S(1)}, f32[1,3,256,128]{3,2,1,0:T(8,128)S(1)}, u32[]{:S(2)}, u32[]{:S(2)}) %collective-permute-start.4) | collective-permute-done | bytes 393248 | tf_op jit(solution)/shard_map/ppermute | solution.py:18
  96.8 0.1 bitcast_add_fusion
  96.9 2.5 %collective-permute-start.6 = (f32[1,256,128]{2,1,0:T(8,128)S(1)}, f32[1,256,128]{2,1,0:T(8,128)S(1)}, u32[]{:S(2)}, u32[]{:S(2)}) collective-permute-start(f32[1,256,128]{2,1,0:T(8,128)S(1)} %get-tuple-element.16), channel_id=1, source_target_pairs={{0,1},{1,2},{2,3},{3,4},{4,5},{5,6},{6,7},{7,0},{8,9},{9,10},{10,1... | collective-permute-start | bytes 393224 | tf_op jit(solution)/shard_map/ppermute | solution.py:18
  99.4 1.4 fusion.11
  100.9 43.6 %psum.7 = f32[3,16,128]{2,1,0:T(8,128)} all-reduce(f32[3,16,128]{2,1,0:T(8,128)S(1)} %pad_maximum_fusion.4), channel_id=1, replica_groups=mesh['gz'=4,'xy'=8] {'gz','xy'}, use_global_device_ids=true, to_apply=%region_8.0 | all-reduce | flops 6144 | bytes 49152 | tf_op jit(solution)/shard_map/psum | solution.py:138
  144.5 0.7 fusion.29
  145.2 3.8 %reduce_sum.89 = f32[3,128,128]{2,1,0:T(8,128)} reduce(f32[32,3,128,128]{3,2,1,0:T(8,128)} %bitcast.173, f32[]{:T(128)} %constant.14.clone.1), dimensions={0}, to_apply=%region_9.0 | reduce | flops 1523712 | bytes 6488068 | tf_op jit(solution)/shard_map/reduce_sum | solution.py:121
  (56 shorter events, 0.3 us)
Async XLA Ops:
  7.2 3.6 %copy-start = (f32[3,16,128]{2,1,0:T(8,128)S(1)}, f32[3,16,128]{2,1,0:T(8,128)}, u32[]{:S(2)}) copy-start(f32[3,16,128]{2,1,0:T(8,128)} %param.12) | copy-start | bytes 73732
  7.2 138.0 %all-gather.3.cloned.1.call-start = ((), (), s32[]{:S(2)}) async-start(), calls=%async_computation | async-start | bytes 6488064 | tf_op jit(solution)/shard_map/all_gather | solution.py:120
  7.2 11.7 %collective-permute-start = (bf16[1,1,256,128]{3,2,1,0:T(8,128)(2,1)}, bf16[1,1,256,128]{3,2,1,0:T(8,128)(2,1)S(1)}, u32[]{:S(2)}, u32[]{:S(2)}) collective-permute-start(bf16[1,1,256,128]{3,2,1,0:T(8,128)(2,1)} %param.11), channel_id=1, source_target_pairs={{0,8},{8,16},{16,24},{24,0},{1,9},{9,17},{17,25},{25,1},{2,10},{10... | collective-permute-start | bytes 196616 | tf_op jit(solution)/shard_map/ppermute | solution.py:18
  7.3 11.7 %collective-permute-start.1 = (bf16[1,1,256,128]{3,2,1,0:T(8,128)(2,1)}, bf16[1,1,256,128]{3,2,1,0:T(8,128)(2,1)S(1)}, u32[]{:S(2)}, u32[]{:S(2)}) collective-permute-start(bf16[1,1,256,128]{3,2,1,0:T(8,128)(2,1)} %param.11), channel_id=1, source_target_pairs={{8,0},{16,8},{24,16},{0,24},{9,1},{17,9},{25,17},{1,25},{10,2},{18... | collective-permute-start | bytes 196616 | tf_op jit(solution)/shard_map/ppermute | solution.py:20
  10.7 7.3 %copy-start.9 = (bf16[1,1,9,128,128]{4,3,2,1,0:T(8,128)(2,1)S(1)}, bf16[1,1,9,128,128]{4,3,2,1,0:T(8,128)(2,1)}, u32[]{:S(2)}) copy-start(bf16[1,1,9,128,128]{4,3,2,1,0:T(8,128)(2,1)} %param.7) | copy-start | bytes 884740
  10.7 8.2 %copy-start.11 = (bf16[1,1,256,128]{3,2,1,0:T(8,128)(2,1)S(1)}, bf16[1,1,256,128]{3,2,1,0:T(8,128)(2,1)}, u32[]{:S(2)}) copy-start(bf16[1,1,256,128]{3,2,1,0:T(8,128)(2,1)} %param.11) | copy-start | bytes 196612
  10.7 10.3 %copy-start.12 = (s32[1,1,32,128]{3,2,1,0:T(8,128)S(1)}, s32[1,1,32,128]{3,2,1,0:T(8,128)}, u32[]{:S(2)}) copy-start(s32[1,1,32,128]{3,2,1,0:T(8,128)} %param.9) | copy-start | bytes 49156
  19.0 11.0 %collective-permute-start.2 = (bf16[3,1,256,128]{3,2,1,0:T(8,128)(2,1)S(1)}, bf16[3,1,256,128]{3,2,1,0:T(8,128)(2,1)S(1)}, u32[]{:S(2)}, u32[]{:S(2)}) collective-permute-start(bf16[3,1,256,128]{3,2,1,0:T(8,128)(2,1)S(1)} %constant_dynamic-update-slice_fusion.9), channel_id=1, source_target_pairs={{0,1},{1,2},{2,3},{3,4},{4,5},{5,6},{6,7},{7,0},{8,9},{9,10},{10,1... | collective-permute-start | bytes 589832 | tf_op jit(solution)/shard_map/ppermute | solution.py:18
  20.6 9.4 %collective-permute-start.3 = (bf16[3,1,256,128]{3,2,1,0:T(8,128)(2,1)S(1)}, bf16[3,1,256,128]{3,2,1,0:T(8,128)(2,1)S(1)}, u32[]{:S(2)}, u32[]{:S(2)}) collective-permute-start(bf16[3,1,256,128]{3,2,1,0:T(8,128)(2,1)S(1)} %constant_dynamic-update-slice_fusion.9), channel_id=1, source_target_pairs={{1,0},{2,1},{3,2},{4,3},{5,4},{6,5},{7,6},{0,7},{9,8},{10,9},{11,1... | collective-permute-start | bytes 589832 | tf_op jit(solution)/shard_map/ppermute | solution.py:20
  47.4 2.0 %copy-start.10 = (bf16[3,128,128]{2,1,0:T(8,128)(2,1)S(1)}, bf16[3,128,128]{2,1,0:T(8,128)(2,1)}, u32[]{:S(2)}) copy-start(bf16[3,128,128]{2,1,0:T(8,128)(2,1)} %param.13) | copy-start | bytes 294916
  49.4 3.6 %copy-start.8 = (f32[1,1,9,128,128]{4,3,2,1,0:T(8,128)S(1)}, f32[1,1,9,128,128]{4,3,2,1,0:T(8,128)}, u32[]{:S(2)}) copy-start(f32[1,1,9,128,128]{4,3,2,1,0:T(8,128)} %convert_element_type.43) | copy-start | bytes 1769476
  55.1 5.5 %copy-start.7 = (f32[1,32,128,128]{3,2,0,1:T(8,128)S(1)}, f32[1,32,128,128]{3,2,0,1:T(8,128)}, u32[]{:S(2)}) copy-start(f32[1,32,128,128]{3,2,0,1:T(8,128)} %get-tuple-element.10) | copy-start | bytes 6291460
  55.2 5.4 %copy-start.5 = (f32[1,32,128,128]{3,2,0,1:T(8,128)S(1)}, f32[1,32,128,128]{3,2,0,1:T(8,128)}, u32[]{:S(2)}) copy-start(f32[1,32,128,128]{3,2,0,1:T(8,128)} %get-tuple-element.5) | copy-start | bytes 6291460
  55.2 5.4 %copy-start.6 = (f32[1,32,128,128]{3,2,0,1:T(8,128)S(1)}, f32[1,32,128,128]{3,2,0,1:T(8,128)}, u32[]{:S(2)}) copy-start(f32[1,32,128,128]{3,2,0,1:T(8,128)} %get-tuple-element.9) | copy-start | bytes 6291460
  57.4 5.7 %copy-start.1 = (f32[32,128,128]{2,1,0:T(8,128)}, f32[32,128,128]{2,1,0:T(8,128)S(1)}, u32[]{:S(2)}) copy-start(f32[32,128,128]{2,1,0:T(8,128)S(1)} %multiply_reduce_fusion.2) | copy-start | bytes 6291460
  60.6 2.5 %copy-start.3 = (f32[32,128,128]{2,1,0:T(8,128)}, f32[32,128,128]{2,1,0:T(8,128)S(1)}, u32[]{:S(2)}) copy-start(f32[32,128,128]{2,1,0:T(8,128)S(1)} %multiply_reduce_fusion) | copy-start | bytes 6291460
  86.0 1.9 %copy-start.2 = (f32[32,128,128]{2,1,0:T(8,128)S(1)}, f32[32,128,128]{2,1,0:T(8,128)}, u32[]{:S(2)}) copy-start(f32[32,128,128]{2,1,0:T(8,128)} %copy-done.1) | copy-start | bytes 6291460
  86.1 10.7 %collective-permute-start.4 = (f32[1,3,256,128]{3,2,1,0:T(8,128)S(1)}, f32[1,3,256,128]{3,2,1,0:T(8,128)S(1)}, u32[]{:S(2)}, u32[]{:S(2)}) collective-permute-start(f32[1,3,256,128]{3,2,1,0:T(8,128)S(1)} %bitcast.176), channel_id=1, source_target_pairs={{0,8},{8,16},{16,24},{24,0},{1,9},{9,17},{17,25},{25,1},{2,10},{10... | collective-permute-start | bytes 1179656 | tf_op jit(solution)/shard_map/ppermute | solution.py:18
  86.2 10.6 %collective-permute-start.5 = (f32[1,3,256,128]{3,2,1,0:T(8,128)S(1)}, f32[1,3,256,128]{3,2,1,0:T(8,128)S(1)}, u32[]{:S(2)}, u32[]{:S(2)}) collective-permute-start(f32[1,3,256,128]{3,2,1,0:T(8,128)S(1)} %bitcast.175), channel_id=1, source_target_pairs={{8,0},{16,8},{24,16},{0,24},{9,1},{17,9},{25,17},{1,25},{10,2},{18... | collective-permute-start | bytes 1179656 | tf_op jit(solution)/shard_map/ppermute | solution.py:20
  87.9 1.6 %copy-start.4 = (f32[32,128,128]{2,1,0:T(8,128)S(1)}, f32[32,128,128]{2,1,0:T(8,128)}, u32[]{:S(2)}) copy-start(f32[32,128,128]{2,1,0:T(8,128)} %copy-done.3) | copy-start | bytes 6291460
  96.9 47.6 %collective-permute-start.6 = (f32[1,256,128]{2,1,0:T(8,128)S(1)}, f32[1,256,128]{2,1,0:T(8,128)S(1)}, u32[]{:S(2)}, u32[]{:S(2)}) collective-permute-start(f32[1,256,128]{2,1,0:T(8,128)S(1)} %get-tuple-element.16), channel_id=1, source_target_pairs={{0,1},{1,2},{2,3},{3,4},{4,5},{5,6},{6,7},{7,0},{8,9},{9,10},{10,1... | collective-permute-start | bytes 393224 | tf_op jit(solution)/shard_map/ppermute | solution.py:18
  99.4 45.1 %collective-permute-start.7 = (f32[1,256,128]{2,1,0:T(8,128)S(1)}, f32[1,256,128]{2,1,0:T(8,128)S(1)}, u32[]{:S(2)}, u32[]{:S(2)}) collective-permute-start(f32[1,256,128]{2,1,0:T(8,128)S(1)} %get-tuple-element.17), channel_id=1, source_target_pairs={{1,0},{2,1},{3,2},{4,3},{5,4},{6,5},{7,6},{0,7},{9,8},{10,9},{11,1... | collective-permute-start | bytes 393224 | tf_op jit(solution)/shard_map/ppermute | solution.py:20
Sparse Core Ops, SparseCore 0:
  54.7 74.6 all-gather.2
